TPU v7x, 512 devices: a whole 4x4x16 slice. The times are simulated.
512 devices in a mesh: ens: 8 (over y_lo, x), slab: 64 (over y_hi, z, core).
Axes of the slice: x: 4, y: 4 (y_hi: 2, y_lo: 2; y = y_hi * 2 + y_lo), z: 16, core: 2. Of those that a mesh axis runs over, the one named last changes fastest.
Arguments:
- state: float32 [64, 64, 1024], P('slab'), may hold values from -6 to 6
- face_coefs: bfloat16 [2, 64, 64, 1024], P(None, 'slab'), may hold values from 0.019897461 to 0.19921875
- codes: int32 [8], P('ens'), may hold values from 0 to 999999
- acoustic_inv: float32 [64, 64, 64], P('slab')
- bounds: int32 [5], replicated, may hold values from 0 to 64, as said below
- land_mask: int32 [64, 1024], P('slab'), may hold values 0 or 1
- target: bfloat16 [64, 64, 1024], P(None, 'slab'), may hold values from -6 to 6
- w_in: bfloat16 [64, 1024], replicated, may hold values from -0.75 to 0.75
- bias_in: float32 [1024], replicated, may hold values from -3 to 3
- land_weight: float32 [1024], replicated, may hold values from -4 to 4
- w_out: bfloat16 [1024, 64], replicated, may hold values from -0.1875 to 0.1875
- bias_out: float32 [64], replicated, may hold values from -3 to 3
Outputs:
- upd_in: float32 [64, 1024], replicated
- upd_out: float32 [1024, 64], replicated
- grad_state: float32 [64, 64, 1024], P('slab')
Inputs may be any that keep to these rules, and one draw needn't show every extreme that they name: bounds[0] = 0 and bounds[4] = 64; the entries rise strictly.
All inputs are finite; a program needn't handle non-finite values. No bound on the sum of `land_mask` on one device may be relied on, other than what follows from the above.
Results may differ from a plain program's by a relative error of at most 0.0004.
The roundings to bfloat16 on the way count: a program that leaves them out, or rounds other values in their place, can miss the bound.
Values sent between devices are 32-bit elements; how exact they have to be, the bound alone decides.
A program may use at most 64 MiB of HBM per device.

v0:
```python
import jax
import jax.numpy as jnp
from jax import lax
from jax.sharding import PartitionSpec as P


def noise(code, cell):
    mult = code % 251 + 2
    first = (mult * (cell % 65521) + 12345) % 65521
    second = (first * 31337 + mult) % 65521
    return second.astype(jnp.float32) / 65521.0 - 0.5


def diffuse(field, east, north):
    flux_x = east * (jnp.roll(field, -1, axis=2) - field)
    step_y = jnp.concatenate([field[:, 1:] - field[:, :-1], jnp.zeros_like(field[:, :1])], axis=1)
    flux_y = north * step_y
    lower = jnp.concatenate([jnp.zeros_like(flux_y[:, :1]), flux_y[:, :-1]], axis=1)
    return field + flux_x - jnp.roll(flux_x, 1, axis=2) + flux_y - lower


def column_step(
    x_row, land_row, target_row, solve_row, w_in, bias_in, land_weight, w_out, bias_out, scale
):
    pre = lax.dot_general(w_in, x_row, (((0,), (0,)), ((), ())), preferred_element_type=jnp.float32)
    pre = pre + bias_in[:, None] + land_weight[:, None] * land_row[None, :]
    sig = jax.nn.sigmoid(pre)
    hidden = (pre * sig).astype(jnp.bfloat16)
    out = lax.dot_general(
        w_out, hidden, (((0,), (0,)), ((), ())), preferred_element_type=jnp.float32
    )
    out = out + bias_out[:, None]
    d_out = ((out - target_row.astype(jnp.float32)) * scale).astype(jnp.bfloat16)
    g_out = lax.dot_general(
        hidden, d_out, (((1,), (1,)), ((), ())), preferred_element_type=jnp.float32
    )
    d_hidden = jnp.dot(w_out, d_out, preferred_element_type=jnp.float32)
    d_pre = (d_hidden * sig * (1.0 + pre * (1.0 - sig))).astype(jnp.bfloat16)
    g_in = lax.dot_general(
        x_row, d_pre, (((1,), (1,)), ((), ())), preferred_element_type=jnp.float32
    )
    d_x = jnp.dot(w_in, d_pre, preferred_element_type=jnp.float32)
    d_h = lax.dot_general(solve_row, d_x, (((0,), (0,)), ((), ())), precision=lax.Precision.HIGHEST)
    return (g_in, g_out, d_h)


def normalized(grad):
    return grad / jnp.sqrt(jnp.mean(grad * grad) + 1e-06)


def on_device(
    state,
    face_coefs,
    codes,
    acoustic_inv,
    bounds,
    land_mask,
    target,
    w_in,
    bias_in,
    land_weight,
    w_out,
    bias_out,
):
    lev_local, lat_count, lon_count = state.shape
    level_count = w_in.shape[0]
    hidden_count = w_in.shape[1]
    lat_local = land_mask.shape[0]
    block_count = bounds.shape[0] - 1
    east = face_coefs[0].astype(jnp.float32)
    north = face_coefs[1].astype(jnp.float32)
    first_level = lax.axis_index("slab") * lev_local
    level_ids = first_level + jnp.arange(lev_local, dtype=jnp.int32)
    lat_ids = jnp.arange(lat_count, dtype=jnp.int32)
    lon_ids = jnp.arange(lon_count, dtype=jnp.int32)
    cell = (level_ids[:, None, None] * lat_count + lat_ids[None, :, None]) * lon_count + lon_ids[
        None, None, :
    ]
    fresh = diffuse(state + noise(codes[0], cell), east, north)
    columns = lax.all_to_all(fresh, "slab", split_axis=1, concat_axis=0, tiled=True)
    level = jnp.arange(level_count, dtype=jnp.int32)
    block = jnp.sum((level[:, None] >= bounds[None, 1:block_count]).astype(jnp.int32), axis=1)
    couple = (block[:, None] == block[None, :]).astype(jnp.float32)
    solve_mat = acoustic_inv * couple[None]
    land = land_mask.astype(jnp.float32)
    scale = 1.0 / lax.axis_size("ens")

    def per_row(row, carry):
        acc_in, acc_out, back = carry
        source = lax.dynamic_index_in_dim(columns, row, 1, keepdims=False)
        solve_row = lax.dynamic_index_in_dim(solve_mat, row, 0, keepdims=False)
        x_row = jnp.dot(solve_row, source, precision=lax.Precision.HIGHEST).astype(jnp.bfloat16)
        land_row = lax.dynamic_index_in_dim(land, row, 0, keepdims=False)
        target_row = lax.dynamic_index_in_dim(target, row, 1, keepdims=False)
        part_in, part_out, d_h = column_step(
            x_row,
            land_row,
            target_row,
            solve_row,
            w_in,
            bias_in,
            land_weight,
            w_out,
            bias_out,
            scale,
        )
        back = d_h[:, None, :]
        return (acc_in + part_in, acc_out + part_out, back)

    start = (
        jnp.zeros((level_count, hidden_count), jnp.float32),
        jnp.zeros((hidden_count, level_count), jnp.float32),
        jnp.zeros((level_count, lat_local, lon_count), jnp.float32),
    )
    g_in, g_out, back = lax.fori_loop(0, lat_local, per_row, start)
    g_in, g_out = lax.psum((g_in, g_out), ("ens", "slab"))
    returned = lax.all_to_all(back, "slab", split_axis=0, concat_axis=1, tiled=True)
    summed = lax.psum(returned, "ens")
    grad_state = diffuse(summed, east, north)
    return (normalized(g_in), normalized(g_out), grad_state)


def solution(mesh):
    placed = (
        P("slab", None, None),
        P(None, "slab", None, None),
        P("ens"),
        P("slab", None, None),
        P(),
        P("slab", None),
        P(None, "slab", None),
        P(),
        P(),
        P(),
        P(),
        P(),
    )
    return jax.shard_map(
        on_device,
        mesh=mesh,
        in_specs=placed,
        out_specs=(P(), P(), P("slab", None, None)),
        check_vma=False,
    )
```

profile of v0, /device:TPU:1, one launch (start us, length us, event | category | flops | bytes accessed | tf_op | source)
XLA Modules:
  0.0 648.9 jit_solution(9690819280671128844)
XLA Ops:
  8.8 4.9 fusion.15
  14.5 1.0 fusion.36
  15.5 5.8 fusion.16
  21.5 5.2 fusion.18
  26.7 19.8 %all-to-all-start = ((f32[1,64,1024]{2,0,1:T(1,128)}), f32[1,64,1024]{2,0,1:T(1,128)S(1)}, u32[]{:S(2)}, u32[]{:S(2)}) async-start(f32[1,64,1024]{2,0,1:T(1,128)} %fusion.18), calls=%async_computation | async-start | bytes 524288 | tf_op jit(solution)/shard_map/all_to_all | solution.py:80
  46.7 23.6 %all-to-all-done = f32[1,64,1024]{2,0,1:T(1,128)S(1)} async-done(((f32[1,64,1024]{2,0,1:T(1,128)}), f32[1,64,1024]{2,0,1:T(1,128)S(1)}, u32[]{:S(2)}, u32[]{:S(2)}) %all-to-all-start) | async-done | bytes 262176 | tf_op jit(solution)/shard_map/all_to_all | solution.py:80
  70.7 1.4 multiply_convert_fusion
  72.2 0.8 fusion.5
  73.5 2.1 fusion.1
  76.9 1.0 copy.23
  77.8 4.2 all-to-all-start.1
  82.1 2.8 fusion.39
  84.8 1.2 fusion.37
  86.3 461.0 %all-reduce.10.cloned.1.call-done = (f32[64,1024]{1,0:T(8,128)}, f32[1024,64]{0,1:T(8,128)}) async-done(((f32[64,1024]{1,0:T(8,128)}, f32[1024,64]{0,1:T(8,128)}), (f32[64,1024]{1,0:T(8,128)}, f32[1024,64]{0,1:T(8,128)})) %all-reduce.10.cloned.1.call-update) | async-done | bytes 524304 | tf_op jit(solution)/shard_map/psum | solution.py:116
  547.3 1.6 multiply_reduce_fusion.1
  549.6 1.7 broadcast_divide_fusion.1
  552.0 1.6 multiply_reduce_fusion
  554.3 1.7 broadcast_divide_fusion
  556.0 77.5 %all-reduce.8.cloned.1.call-done = f32[1,64,1024]{2,0,1:T(1,128)} async-done(((f32[1,64,1024]{2,0,1:T(1,128)}), f32[1,64,1024]{2,0,1:T(1,128)}) %all-reduce.8.cloned.1.call-update) | async-done | bytes 262160 | tf_op jit(solution)/shard_map/psum | solution.py:118
  633.5 1.3 slice_subtract_fusion
  635.1 0.8 slice.80
  635.9 1.6 slice.79
  637.5 1.4 fusion.19
  639.0 1.7 fusion.21
  (45 shorter events, 5.5 us)
Async XLA Ops:
  8.0 62.7 %copy-start = (bf16[64,1024]{1,0:T(8,128)(2,1)S(1)}, bf16[64,1024]{1,0:T(8,128)(2,1)}, u32[]{:S(2)}) copy-start(bf16[64,1024]{1,0:T(8,128)(2,1)} %param.19) | copy-start | bytes 393220
  8.0 13.5 %copy-start.2 = (f32[1,64,1024]{2,1,0:T(8,128)S(1)}, f32[1,64,1024]{2,1,0:T(8,128)}, u32[]{:S(2)}) copy-start(f32[1,64,1024]{2,1,0:T(8,128)} %param.12) | copy-start | bytes 786436
  8.0 38.5 %copy-start.11 = (s32[5]{0:T(128)S(1)}, s32[5]{0:T(128)}, u32[]{:S(2)}) copy-start(s32[5]{0:T(128)} %param.16) | copy-start | bytes 64
  8.0 38.5 %copy-start.7 = (s32[1,1024]{1,0:T(1,128)S(1)}, s32[1,1024]{1,0:T(1,128)}, u32[]{:S(2)}) copy-start(s32[1,1024]{1,0:T(1,128)} %param.17) | copy-start | bytes 12292
  8.0 62.2 %copy-start.4 = (f32[1,64,64]{2,1,0:T(8,128)S(1)}, f32[1,64,64]{2,1,0:T(8,128)}, u32[]{:S(2)}) copy-start(f32[1,64,64]{2,1,0:T(8,128)} %param.15) | copy-start | bytes 49156
  8.1 62.6 %copy-start.9 = (f32[1024]{0:T(1024)S(1)}, f32[1024]{0:T(1024)}, u32[]{:S(2)}) copy-start(f32[1024]{0:T(1024)} %param.21) | copy-start | bytes 12292
  8.1 62.6 %copy-start.10 = (f32[1024]{0:T(1024)S(1)}, f32[1024]{0:T(1024)}, u32[]{:S(2)}) copy-start(f32[1024]{0:T(1024)} %param.20) | copy-start | bytes 12292
  26.7 43.5 %all-to-all-start = ((f32[1,64,1024]{2,0,1:T(1,128)}), f32[1,64,1024]{2,0,1:T(1,128)S(1)}, u32[]{:S(2)}, u32[]{:S(2)}) async-start(f32[1,64,1024]{2,0,1:T(1,128)} %fusion.18), calls=%async_computation | async-start | bytes 524288 | tf_op jit(solution)/shard_map/all_to_all | solution.py:80
  70.7 1.5 copy-start.5
  70.7 1.5 copy-start.6
  70.7 1.5 copy-start.8
  72.1 1.3 copy-start.1
  77.8 473.4 %all-to-all-start.1 = ((f32[64,1,1024]{2,1,0:T(1,128)}), f32[64,1,1024]{2,1,0:T(1,128)S(1)}, u32[]{:S(2)}, u32[]{:S(2)}) async-start(f32[64,1,1024]{2,1,0:T(1,128)} %copy.23), calls=%async_computation.1 | async-start | bytes 524288 | tf_op jit(solution)/shard_map/all_to_all | solution.py:117
  82.0 465.3 %all-reduce.10.cloned.1.call-start = ((), (), s32[]{:S(2)}) async-start(), calls=%async_computation.3 | async-start | bytes 1048576 | tf_op jit(solution)/shard_map/psum | solution.py:116
  86.0 547.4 %all-reduce.8.cloned.1.call-start = ((), (), s32[]{:S(2)}) async-start(), calls=%async_computation.2 | async-start | bytes 524288 | tf_op jit(solution)/shard_map/psum | solution.py:118
  551.3 0.7 copy-start.3
Sparse Core Ops, SparseCore 0:
  88.9 458.2 all-reduce.9
Sparse Core Ops, SparseCore 1:
  552.1 81.4 all-reduce.7
where the time goes:
time: 653 us; the launch traced here: 649 us
  waiting for transfers between devices  562 us (86%)
  other arithmetic  27.4 us (4%)
  starting transfers between devices  24.2 us (4%)
  between operations  17.9 us (3%)
  matrix products  9.94 us (2%)
  local copies, waits for them, and re-layouts  7.28 us (1%)
    psum x1, waiting for transfers between devices, on_device(): g_in, g_out = lax.psum((g_in, g_out), ('ens', 'slab'))  461 us
    psum x1, waiting for transfers between devices, on_device(): summed = lax.psum(returned, 'ens')  77.5 us
    all_to_all x1, waiting for transfers between devices, on_device(): lax.all_to_all(fresh, 'slab', split_axis=1, concat_axis=0, tiled=True)  23.6 us
    all_to_all x1, starting transfers between devices, on_device(): lax.all_to_all(fresh, 'slab', split_axis=1, concat_axis=0, tiled=True)  19.8 us
  transfers between devices with their start and end apart: 4, of which 3 were waited for; matrix products, arithmetic and copies ran while one was open for 2% of the time, Pallas kernels for 0%

commit v1 on v0

v1 whole, which is shorter than its diff:
```python
import functools

import jax
import jax.numpy as jnp
from jax import lax
from jax.experimental import pallas as pl
from jax.experimental.pallas import tpu as pltpu
from jax.sharding import PartitionSpec as P

MESH = pl.DeviceIdType.MESH
LANES = 128
PRIME = 65521


def reduced(value):
    value = (value & 65535) + 15 * (value >> 16)
    return value


def below_prime(value):
    return jnp.where(value >= PRIME, value - PRIME, value)


def noise(mult, base, first_row, rows, lons):
    shape = (rows, lons)
    row = lax.broadcasted_iota(jnp.int32, shape, 0) + first_row
    cell = below_prime(row * lons + lax.broadcasted_iota(jnp.int32, shape, 1) + base)
    first = below_prime(reduced(mult * cell + 12345))
    second = below_prime(reduced(reduced(first * 31337 + mult)))
    return second.astype(jnp.float32) * (1.0 / PRIME) - 0.5


def prepare_north(coef_ref, north):
    lats, lons = coef_ref.shape[1:]
    north[0:8, :] = jnp.zeros((8, lons), jnp.float32)
    for start in range(0, lats, 16):
        part = coef_ref[1, start : start + 16, :].astype(jnp.float32)
        if start + 16 >= lats:
            row = lax.broadcasted_iota(jnp.int32, part.shape, 0) + start
            part = jnp.where(row < lats - 1, part, 0.0)
        north[8 + start : 8 + start + part.shape[0], :] = part


def diffuse(field, coef_ref, north, emit):
    lats, lons = coef_ref.shape[1:]
    step = min(16, lats)
    for start in range(0, lats, step):
        here = field[8 + start : 8 + start + step, :]
        ahead = field[9 + start : 9 + start + step, :]
        behind = field[7 + start : 7 + start + step, :]
        east = coef_ref[0, start : start + step, :].astype(jnp.float32)
        flux_x = east * (pltpu.roll(here, lons - 1, 1) - here)
        flux_y = north[8 + start : 8 + start + step, :] * (ahead - here)
        lower = north[7 + start : 7 + start + step, :] * (here - behind)
        emit(start, step, here + flux_x - pltpu.roll(flux_x, 1, 1) + flux_y - lower)


def offset_of(step, count):
    half = step // 2 + 1
    return jnp.where(step % 2 == 0, half, count - half)


def for_peers(count, me, body):
    def one(step, carry):
        body(lax.rem(me + offset_of(step, count), count))
        return carry

    lax.fori_loop(0, count - 1, one, 0)


def wait_bytes(ref, sem):
    pltpu.make_async_copy(ref, ref, sem).wait()


def rows_of(index, size):
    return pl.ds(pl.multiple_of(index * size, size), size)


def spread_kernel(
    members, slabs, state_ref, coef_ref, code_ref, out_ref, field, north, send, recv, send_sem, recv_sem
):
    ens, slab = lax.axis_index("ens"), lax.axis_index("slab")
    lats, lons = state_ref.shape
    blocks = lons // LANES
    barrier = pltpu.get_barrier_semaphore()
    for_peers(
        slabs,
        slab,
        lambda d: pl.semaphore_signal(barrier, inc=1, device_id=(ens, d), device_id_type=MESH),
    )
    mult = lax.rem(code_ref[0], 251) + 2
    base = lax.rem(slab * (lats * lons), PRIME)
    field[0:8, :] = jnp.zeros((8, lons), jnp.float32)
    field[8 + lats : 16 + lats, :] = jnp.zeros((8, lons), jnp.float32)
    for start in range(0, lats, 8):
        field[8 + start : 16 + start, :] = state_ref[start : start + 8, :] + noise(
            mult, base, start, 8, lons
        )
    prepare_north(coef_ref, north)

    def emit(start, rows, value):
        for j in range(blocks):
            send[pl.ds(start * blocks + j, rows, stride=blocks), :] = value[
                :, j * LANES : (j + 1) * LANES
            ]

    diffuse(field, coef_ref, north, emit)
    pl.semaphore_wait(barrier, slabs - 1)

    def put(d):
        pltpu.make_async_remote_copy(
            src_ref=send.at[rows_of(d, blocks)],
            dst_ref=recv.at[rows_of(slab, blocks)],
            send_sem=send_sem,
            recv_sem=recv_sem,
            device_id=(ens, d),
            device_id_type=MESH,
        ).start()

    for_peers(slabs, slab, put)
    recv[rows_of(slab, blocks), :] = send[rows_of(slab, blocks), :]
    others = pl.ds(0, (slabs - 1) * blocks)
    wait_bytes(recv.at[others], recv_sem)
    out_ref[...] = recv[...]
    wait_bytes(send.at[others], send_sem)


def parts_of(value):
    high = value.astype(jnp.bfloat16).astype(jnp.float32)
    rest = value - high
    middle = rest.astype(jnp.bfloat16).astype(jnp.float32)
    return high, middle, rest - middle


def contract(a, b, dims, **kw):
    return lax.dot_general(a, b, (dims, ((), ())), preferred_element_type=jnp.float32, **kw)


def network_kernel(
    members,
    cols_ref,
    solve_ref,
    bounds_ref,
    land_ref,
    target_ref,
    w_in_ref,
    bias_in_ref,
    land_weight_ref,
    w_out_ref,
    bias_out_ref,
    back_ref,
    grads_ref,
    w_aug,
    w_back,
    x_aug,
    shift,
    z_s,
    slope,
    dy_s,
    da_s,
):
    levels, lons = target_ref.shape
    hidden = w_in_ref.shape[1]
    blocks = lons // LANES
    pad = w_aug.shape[1]
    hb = min(128, hidden)
    cb = min(256, lons)
    row = lax.broadcasted_iota(jnp.int32, (levels, levels), 0)
    col = lax.broadcasted_iota(jnp.int32, (levels, levels), 1)
    row_block = jnp.zeros((levels, levels), jnp.int32)
    col_block = jnp.zeros((levels, levels), jnp.int32)
    for j in range(1, bounds_ref.shape[0] - 1):
        row_block += (row >= bounds_ref[j]).astype(jnp.int32)
        col_block += (col >= bounds_ref[j]).astype(jnp.int32)
    solve = jnp.where(row_block == col_block, solve_ref[...], 0.0)
    bias = parts_of(bias_in_ref[...] * 0.5)
    land_w = parts_of(land_weight_ref[...] * 0.5)
    land = land_ref[...].astype(jnp.float32)
    extra = pad - levels
    extra_row = lax.broadcasted_iota(jnp.int32, (extra, hidden), 0)
    tail = jnp.zeros((extra, hidden), jnp.float32)
    for k, part in enumerate(bias + land_w):
        tail = jnp.where(extra_row == k, part, tail)
    whole = jnp.concatenate([w_in_ref[...].astype(jnp.float32) * 0.5, tail], axis=0)
    w_aug[...] = whole.T.astype(jnp.bfloat16)
    spread = jnp.concatenate(
        [w_out_ref[...].astype(jnp.float32) * 0.5, jnp.zeros((extra, hidden), jnp.float32)], axis=0
    )
    w_back[...] = spread.T.astype(jnp.bfloat16)
    lon_row = lax.broadcasted_iota(jnp.int32, (extra, lons), 0)
    ones = jnp.where(lon_row < 3, 1.0, jnp.where(lon_row < 6, land, 0.0))
    x_aug[levels:, :] = ones.astype(jnp.bfloat16)
    bias_col = jnp.sum(jnp.where(row == col, bias_out_ref[...], 0.0), axis=1, keepdims=True)
    shift[...] = bias_col - target_ref[...].astype(jnp.float32)
    dy_s[levels:, :] = jnp.zeros((extra, lons), jnp.bfloat16)
    highest = lax.Precision.HIGHEST
    for start in range(0, lons, cb):
        here = slice(start, start + cb)
        h = jnp.concatenate(
            [
                cols_ref[pl.ds(j, levels, stride=blocks), :]
                for j in range(start // LANES, (start + cb) // LANES)
            ],
            axis=1,
        )
        x = contract(solve, h, ((1,), (0,)), precision=highest).astype(jnp.bfloat16)
        x_aug[0:levels, here] = x
        x_all = x_aug[:, here]
        for k in range(0, hidden, hb):
            half = contract(w_aug[k : k + hb, :], x_all, ((1,), (0,)))
            t = jnp.tanh(half)
            both = half * t
            z_s[k : k + hb, here] = (half + both).astype(jnp.bfloat16)
            slope[k : k + hb, here] = (1.0 + t) * (1.0 + half - both)
        out = contract(w_out_ref[...], z_s[:, here], ((1,), (0,)))
        dy = ((out + shift[:, here]) * (1.0 / members)).astype(jnp.bfloat16)
        dy_s[0:levels, here] = dy
        dy_all = dy_s[:, here]
        for k in range(0, hidden, hb):
            dz = contract(w_back[k : k + hb, :], dy_all, ((1,), (0,)))
            da_s[k : k + hb, here] = (dz * slope[k : k + hb, here]).astype(jnp.bfloat16)
        dx = contract(w_in_ref[...], da_s[:, here], ((1,), (0,)))
        dh = contract(solve, dx, ((0,), (0,)), precision=highest)
        for j in range(cb // LANES):
            first = (start // LANES + j) * levels
            back_ref[first : first + levels, :] = dh[:, j * LANES : (j + 1) * LANES]
    grads_ref[0] = contract(x_aug[0:levels, :], da_s[...], ((1,), (1,)))
    grads_ref[1] = contract(dy_s[0:levels, :], z_s[...], ((1,), (1,)))


def reduce_kernel(
    members,
    slabs,
    back_ref,
    grads_ref,
    field_ref,
    total_ref,
    back_in,
    pair_in,
    pair_sum,
    grad_in,
    level_out,
    level_in,
    piece_out,
    piece_in,
    piece_sum,
    piece_all,
    field_in,
    rows_out,
    rows_all,
    pair_all,
    send_sem,
    recv_sem,
):
    ens, slab = lax.axis_index("ens"), lax.axis_index("slab")
    core, place = lax.rem(slab, 2), slab // 2
    twin = slab + 1 - 2 * core
    places = slabs // 2
    levels, lons = grads_ref.shape[1:]
    chunk = back_ref.shape[0] // members
    rows = levels // members
    barrier = pltpu.get_barrier_semaphore()

    def greet(device):
        pl.semaphore_signal(barrier, inc=1, device_id=device, device_id_type=MESH)

    for_peers(members, ens, lambda e: greet((e, slab)))
    for_peers(slabs, slab, lambda d: greet((ens, d)))

    def put(k, src, dst, device):
        pltpu.make_async_remote_copy(
            src_ref=src,
            dst_ref=dst,
            send_sem=send_sem.at[k],
            recv_sem=recv_sem.at[k],
            device_id=device,
            device_id_type=MESH,
        ).start()

    pl.semaphore_wait(barrier, members + slabs - 2)
    put(0, grads_ref.at[1 - core], pair_in, (ens, twin))
    for_peers(
        members,
        ens,
        lambda e: put(
            1, back_ref.at[rows_of(e, chunk)], back_in.at[rows_of(ens, chunk)], (e, slab)
        ),
    )
    back_in[rows_of(ens, chunk), :] = back_ref[rows_of(ens, chunk), :]
    wait_bytes(pair_in, recv_sem.at[0])
    pair_sum[...] = grads_ref[core] + pair_in[...]
    for_peers(
        members,
        ens,
        lambda e: put(
            2, pair_sum.at[rows_of(e, rows)], grad_in.at[rows_of(ens, rows)], (e, slab)
        ),
    )
    grad_in[rows_of(ens, rows), :] = pair_sum[rows_of(ens, rows), :]
    wait_bytes(back_in.at[pl.ds(0, (members - 1) * chunk)], recv_sem.at[1])
    total = back_in[0:chunk, :]
    for e in range(1, members):
        total += back_in[e * chunk : (e + 1) * chunk, :]
    for l in range(levels):
        level_out[l] = total[l : l + 1, :]
    for_peers(
        slabs, slab, lambda d: put(3, level_out.at[d], level_in.at[slab], (ens, d))
    )
    level_in[slab] = level_out[slab]
    wait_bytes(grad_in.at[pl.ds(0, (members - 1) * rows)], recv_sem.at[2])
    total = grad_in[0:rows, :]
    for e in range(1, members):
        total += grad_in[e * rows : (e + 1) * rows, :]
    per = rows // 2
    for p in range(places):
        t, s = p // per, p % per
        piece_out[p] = total[2 * s : 2 * s + 2, t * LANES : (t + 1) * LANES]
    for_peers(
        places,
        place,
        lambda q: put(4, piece_out.at[q], piece_in.at[place], (ens, 2 * q + core)),
    )
    piece_in[place] = piece_out[place]
    wait_bytes(level_in.at[pl.ds(0, slabs - 1)], recv_sem.at[3])
    for_peers(members, ens, lambda e: put(5, level_in, field_in.at[ens], (e, slab)))
    field_in[ens] = level_in[...]
    wait_bytes(piece_in.at[pl.ds(0, places - 1)], recv_sem.at[4])
    piece_sum[...] = jnp.sum(piece_in[...], axis=0)
    for_peers(
        places,
        place,
        lambda q: put(6, piece_sum, piece_all.at[place], (ens, 2 * q + core)),
    )
    piece_all[place] = piece_sum[...]
    wait_bytes(piece_all.at[pl.ds(0, places - 1)], recv_sem.at[6])
    for p in range(places):
        t, s = p // per, p % per
        rows_out[2 * s : 2 * s + 2, t * LANES : (t + 1) * LANES] = piece_all[p]
    for_peers(
        members, ens, lambda e: put(7, rows_out, rows_all.at[rows_of(ens, rows)], (e, slab))
    )
    rows_all[rows_of(ens, rows), :] = rows_out[...]
    wait_bytes(rows_all.at[pl.ds(0, (members - 1) * rows)], recv_sem.at[7])
    put(8, rows_all, pair_all, (ens, twin))
    total_ref[core] = rows_all[...]
    wait_bytes(field_in.at[pl.ds(0, members - 1)], recv_sem.at[5])
    for e in range(members):
        field_ref[e] = field_in[e].reshape(levels, LANES)
    wait_bytes(pair_all, recv_sem.at[8])
    total_ref[1 - core] = pair_all[...]
    wait_bytes(grads_ref.at[0], send_sem.at[0])
    wait_bytes(back_in.at[pl.ds(0, (members - 1) * chunk)], send_sem.at[1])
    wait_bytes(grad_in.at[pl.ds(0, (members - 1) * rows)], send_sem.at[2])
    wait_bytes(level_in.at[pl.ds(0, slabs - 1)], send_sem.at[3])
    wait_bytes(piece_in.at[pl.ds(0, places - 1)], send_sem.at[4])
    wait_bytes(field_in.at[pl.ds(0, members - 1)], send_sem.at[5])
    wait_bytes(piece_all.at[pl.ds(0, places - 1)], send_sem.at[6])
    wait_bytes(rows_all.at[pl.ds(0, (members - 1) * rows)], send_sem.at[7])
    wait_bytes(pair_all, send_sem.at[8])


def finish_kernel(field_ref, total_ref, coef_ref, in_ref, out_ref, state_ref, field, north):
    lats, lons = state_ref.shape
    for k, ref in ((0, in_ref), (1, out_ref)):
        grad = total_ref[k]
        square = jnp.sum(jnp.sum(grad * grad, axis=0, keepdims=True), axis=1, keepdims=True)
        ref[...] = grad / jnp.sqrt(square * (1.0 / grad.size) + 1e-06)
    field[0:8, :] = jnp.zeros((8, lons), jnp.float32)
    field[8 + lats : 16 + lats, :] = jnp.zeros((8, lons), jnp.float32)
    for j in range(field_ref.shape[0]):
        field[8 : 8 + lats, j * LANES : (j + 1) * LANES] = field_ref[j]
    prepare_north(coef_ref, north)

    def emit(start, rows, value):
        state_ref[start : start + rows, :] = value

    diffuse(field, coef_ref, north, emit)


def on_device(
    members,
    slabs,
    state,
    face_coefs,
    codes,
    acoustic_inv,
    bounds,
    land_mask,
    target,
    w_in,
    bias_in,
    land_weight,
    w_out,
    bias_out,
):
    _, lats, lons = state.shape
    levels, hidden = w_in.shape
    blocks = lons // LANES
    f32, bf16 = jnp.float32, jnp.bfloat16
    vmem = pl.BlockSpec(memory_space=pltpu.VMEM)
    smem = pl.BlockSpec(memory_space=pltpu.SMEM)
    like = jax.ShapeDtypeStruct
    dma = pltpu.SemaphoreType.DMA
    coefs = face_coefs.reshape(2, lats, lons)
    limit = 40 * 1024 * 1024
    columns = pl.pallas_call(
        functools.partial(spread_kernel, members, slabs),
        out_shape=like((levels * blocks, LANES), f32),
        in_specs=[vmem, vmem, smem],
        out_specs=vmem,
        scratch_shapes=[
            pltpu.VMEM((lats + 16, lons), f32),
            pltpu.VMEM((lats + 8, lons), f32),
            pltpu.VMEM((lats * blocks, LANES), f32),
            pltpu.VMEM((levels * blocks, LANES), f32),
            dma,
            dma,
        ],
        compiler_params=pltpu.CompilerParams(
            collective_id=0, has_side_effects=True, vmem_limit_bytes=limit
        ),
    )(state.reshape(lats, lons), coefs, codes)
    pad = 2 * levels if levels >= 64 else levels + 8
    back, grads = pl.pallas_call(
        functools.partial(network_kernel, members),
        out_shape=(like((blocks * levels, LANES), f32), like((2, levels, hidden), f32)),
        in_specs=[vmem, vmem, smem] + [vmem] * 7,
        out_specs=(vmem, vmem),
        scratch_shapes=[
            pltpu.VMEM((hidden, pad), bf16),
            pltpu.VMEM((hidden, pad), bf16),
            pltpu.VMEM((pad, lons), bf16),
            pltpu.VMEM((levels, lons), f32),
            pltpu.VMEM((hidden, lons), bf16),
            pltpu.VMEM((hidden, lons), f32),
            pltpu.VMEM((pad, lons), bf16),
            pltpu.VMEM((hidden, lons), bf16),
        ],
        compiler_params=pltpu.CompilerParams(vmem_limit_bytes=limit),
    )(
        columns,
        acoustic_inv.reshape(levels, levels),
        bounds,
        land_mask,
        target.reshape(levels, lons),
        w_in,
        bias_in.reshape(1, hidden),
        land_weight.reshape(1, hidden),
        w_out.T,
        bias_out.reshape(1, levels),
    )
    rows = levels // members
    places = slabs // 2
    chunk = levels * blocks // members
    field, total = pl.pallas_call(
        functools.partial(reduce_kernel, members, slabs),
        out_shape=(like((members, levels, LANES), f32), like((2, levels, hidden), f32)),
        in_specs=[vmem, vmem],
        out_specs=(vmem, vmem),
        scratch_shapes=[
            pltpu.VMEM((members * chunk, LANES), f32),
            pltpu.VMEM((levels, hidden), f32),
            pltpu.VMEM((levels, hidden), f32),
            pltpu.VMEM((levels, hidden), f32),
            pltpu.VMEM((levels, 1, LANES), f32),
            pltpu.VMEM((levels, 1, LANES), f32),
            pltpu.VMEM((places, 2, LANES), f32),
            pltpu.VMEM((places, 2, LANES), f32),
            pltpu.VMEM((2, LANES), f32),
            pltpu.VMEM((places, 2, LANES), f32),
            pltpu.VMEM((members, levels, 1, LANES), f32),
            pltpu.VMEM((rows, hidden), f32),
            pltpu.VMEM((levels, hidden), f32),
            pltpu.VMEM((levels, hidden), f32),
            dma((9,)),
            dma((9,)),
        ],
        compiler_params=pltpu.CompilerParams(
            collective_id=1, has_side_effects=True, vmem_limit_bytes=limit
        ),
    )(back, grads)
    upd_in, upd_out, grad_state = pl.pallas_call(
        finish_kernel,
        out_shape=(
            like((levels, hidden), f32),
            like((levels, hidden), f32),
            like((lats, lons), f32),
        ),
        in_specs=[vmem] * 3,
        out_specs=(vmem,) * 3,
        scratch_shapes=[
            pltpu.VMEM((lats + 16, lons), f32),
            pltpu.VMEM((lats + 8, lons), f32),
        ],
        compiler_params=pltpu.CompilerParams(vmem_limit_bytes=limit),
    )(field, total, coefs)
    return upd_in, upd_out.T, grad_state.reshape(state.shape)


def solution(mesh):
    placed = (
        P("slab", None, None),
        P(None, "slab", None, None),
        P("ens"),
        P("slab", None, None),
        P(),
        P("slab", None),
        P(None, "slab", None),
        P(),
        P(),
        P(),
        P(),
        P(),
    )
    return jax.shard_map(
        functools.partial(on_device, mesh.shape["ens"], mesh.shape["slab"]),
        mesh=mesh,
        in_specs=placed,
        out_specs=(P(), P(), P("slab", None, None)),
        check_vma=False,
    )
```

time: 653 us -> 86.8 us (0.13)
  waiting for transfers between devices: 562 us -> 0 us
  Pallas kernels: 0 us -> 83.3 us
  other arithmetic: 27.4 us -> 0 us
  starting transfers between devices: 24.2 us -> 0 us
  between operations: 17.9 us -> 1.44 us
  matrix products: 9.94 us -> 0 us
    psum x2 -> x0, waiting for transfers between devices: 538 us -> none  [the longest x1 461 us: on_device(): g_in, g_out = lax.psum((g_in, g_out), ('ens', 'slab'))]
    pallas_call x0 -> x4, Pallas kernels: none -> 83.3 us  [the longest x1 42.9 us: on_device(): pl.pallas_call(functools.partial(reduce_kernel, members, slabs), out_shap...]
    all_to_all x2 -> x0, starting transfers between devices: 24 us -> none  [the longest x1 19.8 us: on_device(): lax.all_to_all(fresh, 'slab', split_axis=1, concat_axis=0, tiled=True)]
    all_to_all x2 -> x0, waiting for transfers between devices: 23.6 us -> none  [the longest x1 23.6 us: on_device(): lax.all_to_all(fresh, 'slab', split_axis=1, concat_axis=0, tiled=True)]
    dot_general x8 -> x0, matrix products: 9.94 us -> none  [the longest x1 2.78 us: column_step(): lax.dot_general(hidden, d_out, (((1,), (1,)), ((), ())), preferred_elemen...]
    sub x4 -> x0, other arithmetic: 8.35 us -> none  [the longest x2 6.83 us: diffuse(): return field + flux_x - jnp.roll(flux_x, 1, axis=2) + flux_y - lower]
    mul x4 -> x0, other arithmetic: 7.5 us -> none  [the longest x2 7.23 us: diffuse(): flux_x = east * (jnp.roll(field, -1, axis=2) - field)]
  transfers between devices with their start and end apart: 4 -> 0, of which waited for: 3 -> 0; matrix products, arithmetic and copies ran while one was open for 2% -> 0% of each run, Pallas kernels for 0% -> 0%
where the time goes in v1:
time: 86.8 us; the launch traced here: 86.6 us
  Pallas kernels  83.3 us (96%)
  local copies, waits for them, and re-layouts  1.94 us (2%)
  between operations  1.44 us (2%)
    pallas_call x1, Pallas kernels, on_device(): pl.pallas_call(functools.partial(reduce_kernel, members, slabs), out_shap...  42.9 us
    pallas_call x1, Pallas kernels, on_device(): pl.pallas_call(functools.partial(spread_kernel, members, slabs), out_shap...  32.7 us
    pallas_call x1, Pallas kernels, on_device(): pl.pallas_call(functools.partial(network_kernel, members), out_shape=(lik...  6.59 us
    unnamed x24, local copies, waits for them, and re-layouts  1.94 us

profile of v1, /device:TPU:1, one launch (start us, length us, event | category | flops | bytes accessed | tf_op | source)
XLA Modules:
  0.0 86.6 jit_solution(14144688073088886072)
XLA Ops:
  1.3 0.0 copy-start
  1.3 0.9 %copy-done = bf16[2,1,64,1024]{3,2,1,0:T(8,128)(2,1)S(1)} copy-done((bf16[2,1,64,1024]{3,2,1,0:T(8,128)(2,1)S(1)}, bf16[2,1,64,1024]{3,2,1,0:T(8,128)(2,1)}, u32[]{:S(2)}) %copy-start) | copy-done | bytes 262168
  2.2 0.0 copy-start.2
  2.2 0.9 %copy-done.2 = f32[1,64,1024]{2,1,0:T(8,128)S(1)} copy-done((f32[1,64,1024]{2,1,0:T(8,128)S(1)}, f32[1,64,1024]{2,1,0:T(8,128)}, u32[]{:S(2)}) %copy-start.2) | copy-done | bytes 262168
  3.2 0.0 copy-start.7
  3.2 0.0 copy-start.8
  3.2 0.0 copy-start.9
  3.2 0.0 copy-start.10
  3.2 0.0 copy-start.11
  3.2 32.7 %shard_map.139.cols_ref = f32[512,128]{1,0:T(8,128)S(1)} custom-call(f32[64,1024]{1,0:T(8,128)S(1)} %bitcast.12, bf16[2,64,1024]{2,1,0:T(8,128)(2,1)S(1)} %bitcast.10, s32[1]{0:T(128)S(6)} %copy.15.code_ref), custom_call_target="tpu_custom_call" | custom-call | tf_op jit(solution)/shard_map/pallas_call | solution.py:406
  35.9 0.0 copy-done.3
  35.9 0.0 copy-done.4
  36.0 0.0 copy-done.5
  36.0 0.0 copy-done.6
  36.0 0.0 copy-done.7
  36.0 0.0 copy-done.8
  36.0 0.0 copy-done.9
  36.0 0.0 copy-done.10
  36.0 0.0 copy-done.11
  36.0 6.6 %shard_map.140 = (f32[512,128]{1,0:T(8,128)S(1)}, f32[2,64,1024]{2,1,0:T(8,128)S(1)}) custom-call(f32[512,128]{1,0:T(8,128)S(1)} %shard_map.139.cols_ref, f32[64,64]{1,0:T(8,128)S(1)} %bitcast.15, s32[5]{0:T(128)S(1)} %copy-done.10, s32[1,1024]{1,0:T(1,128)S(1)} %copy-done.7, bf16[64,1024]{1,0:T(8,128)(2,1)S(1)} %bitcast.13, bf16[64,1024]{1,0:T(8,128)(2,1)S(1)} %copy-done.4, ...), custom_call_target="tpu_custom_call" | custom-call | tf_op jit(solution)/shard_map/pallas_call | solution.py:424
  42.6 0.0 copy-start.1
  42.6 42.9 %shard_map.141 = (f32[8,64,128]{2,1,0:T(8,128)S(1)}, f32[2,64,1024]{2,1,0:T(8,128)S(1)}) custom-call(f32[512,128]{1,0:T(8,128)S(1)} %get-tuple-element.10.back_ref, f32[2,64,1024]{2,1,0:T(8,128)S(1)} %get-tuple-element.11.grads_ref), custom_call_target="tpu_custom_call" | custom-call | tf_op jit(solution)/shard_map/pallas_call | solution.py:455
  85.5 0.0 copy-done.1
  85.6 1.1 %shard_map.142 = (f32[64,1024]{1,0:T(8,128)}, f32[64,1024]{1,0:T(8,128)}, f32[64,1024]{1,0:T(8,128)}) custom-call(f32[8,64,128]{2,1,0:T(8,128)S(1)} %get-tuple-element.12.field_ref, f32[2,64,1024]{2,1,0:T(8,128)S(1)} %get-tuple-element.13.total_ref, bf16[2,64,1024]{2,1,0:T(8,128)(2,1)S(1)} %bitcast.11), custom_call_target="tpu_custom_call" | custom-call | tf_op jit(solution)/shard_map/pallas_call | solution.py:482
  (4 shorter events, 0.0 us)
Async XLA Ops:
  1.3 1.0 %copy-start = (bf16[2,1,64,1024]{3,2,1,0:T(8,128)(2,1)S(1)}, bf16[2,1,64,1024]{3,2,1,0:T(8,128)(2,1)}, u32[]{:S(2)}) copy-start(bf16[2,1,64,1024]{3,2,1,0:T(8,128)(2,1)} %param.13) | copy-start | bytes 786436
  2.2 0.9 %copy-start.2 = (f32[1,64,1024]{2,1,0:T(8,128)S(1)}, f32[1,64,1024]{2,1,0:T(8,128)}, u32[]{:S(2)}) copy-start(f32[1,64,1024]{2,1,0:T(8,128)} %param.12) | copy-start | bytes 786436
  3.2 32.8 %copy-start.3 = (bf16[64,1,1024]{2,0,1:T(8,128)(2,1)S(1)}, bf16[64,1,1024]{2,0,1:T(8,128)(2,1)}, u32[]{:S(2)}) copy-start(bf16[64,1,1024]{2,0,1:T(8,128)(2,1)} %param.18) | copy-start | bytes 393220
  3.2 32.8 %copy-start.4 = (bf16[64,1024]{1,0:T(8,128)(2,1)S(1)}, bf16[64,1024]{1,0:T(8,128)(2,1)}, u32[]{:S(2)}) copy-start(bf16[64,1024]{1,0:T(8,128)(2,1)} %w_in_ref.1) | copy-start | bytes 393220
  3.2 32.8 %copy-start.5 = (bf16[1024,64]{0,1:T(8,128)(2,1)S(1)}, bf16[1024,64]{0,1:T(8,128)(2,1)}, u32[]{:S(2)}) copy-start(bf16[1024,64]{0,1:T(8,128)(2,1)} %param.22) | copy-start | bytes 393220
  3.2 32.8 %copy-start.6 = (f32[1,64,64]{2,1,0:T(8,128)S(1)}, f32[1,64,64]{2,1,0:T(8,128)}, u32[]{:S(2)}) copy-start(f32[1,64,64]{2,1,0:T(8,128)} %param.15) | copy-start | bytes 49156
  3.2 32.8 %copy-start.7 = (s32[1,1024]{1,0:T(1,128)S(1)}, s32[1,1024]{1,0:T(1,128)}, u32[]{:S(2)}) copy-start(s32[1,1024]{1,0:T(1,128)} %land_ref.1) | copy-start | bytes 12292
  3.2 32.8 %copy-start.8 = (f32[1024]{0:T(1024)S(1)}, f32[1024]{0:T(1024)}, u32[]{:S(2)}) copy-start(f32[1024]{0:T(1024)} %param.20) | copy-start | bytes 12292
  3.2 32.8 %copy-start.9 = (f32[1024]{0:T(1024)S(1)}, f32[1024]{0:T(1024)}, u32[]{:S(2)}) copy-start(f32[1024]{0:T(1024)} %param.21) | copy-start | bytes 12292
  3.2 32.8 %copy-start.10 = (s32[5]{0:T(128)S(1)}, s32[5]{0:T(128)}, u32[]{:S(2)}) copy-start(s32[5]{0:T(128)} %bounds_ref.1) | copy-start | bytes 64
  3.2 32.8 %copy-start.11 = (f32[64]{0:T(128)S(1)}, f32[64]{0:T(128)}, u32[]{:S(2)}) copy-start(f32[64]{0:T(128)} %param.23) | copy-start | bytes 772
  42.6 42.9 %copy-start.1 = (bf16[2,1,64,1024]{3,2,1,0:T(8,128)(2,1)S(1)}, bf16[2,1,64,1024]{3,2,1,0:T(8,128)(2,1)}, u32[]{:S(2)}) copy-start(bf16[2,1,64,1024]{3,2,1,0:T(8,128)(2,1)} %param.13) | copy-start | bytes 786436

commit v2 on v0

v2 whole, which is shorter than its diff:
```python
import functools

import jax
import jax.numpy as jnp
from jax import lax
from jax.experimental import pallas as pl
from jax.experimental.pallas import tpu as pltpu
from jax.sharding import PartitionSpec as P

MESH = pl.DeviceIdType.MESH
LANES = 128
PRIME = 65521


def reduced(value):
    value = (value & 65535) + 15 * (value >> 16)
    return value


def below_prime(value):
    return jnp.where(value >= PRIME, value - PRIME, value)


def noise(mult, base, first_row, rows, lons):
    shape = (rows, lons)
    row = lax.broadcasted_iota(jnp.int32, shape, 0) + first_row
    cell = below_prime(row * lons + lax.broadcasted_iota(jnp.int32, shape, 1) + base)
    first = below_prime(reduced(mult * cell + 12345))
    second = below_prime(reduced(reduced(first * 31337 + mult)))
    return second.astype(jnp.float32) * (1.0 / PRIME) - 0.5


def prepare_north(coef_ref, north):
    lats, lons = coef_ref.shape[1:]
    north[0:8, :] = jnp.zeros((8, lons), jnp.float32)
    for start in range(0, lats, 16):
        part = coef_ref[1, start : start + 16, :].astype(jnp.float32)
        if start + 16 >= lats:
            row = lax.broadcasted_iota(jnp.int32, part.shape, 0) + start
            part = jnp.where(row < lats - 1, part, 0.0)
        north[8 + start : 8 + start + part.shape[0], :] = part


def diffuse(field, coef_ref, north, emit):
    lats, lons = coef_ref.shape[1:]
    step = min(16, lats)
    for start in range(0, lats, step):
        here = field[8 + start : 8 + start + step, :]
        ahead = field[9 + start : 9 + start + step, :]
        behind = field[7 + start : 7 + start + step, :]
        east = coef_ref[0, start : start + step, :].astype(jnp.float32)
        flux_x = east * (pltpu.roll(here, lons - 1, 1) - here)
        flux_y = north[8 + start : 8 + start + step, :] * (ahead - here)
        lower = north[7 + start : 7 + start + step, :] * (here - behind)
        emit(start, step, here + flux_x - pltpu.roll(flux_x, 1, 1) + flux_y - lower)


def offset_of(step, count):
    half = step // 2 + 1
    return jnp.where(step % 2 == 0, half, count - half)


def for_peers(count, me, body):
    def one(step, carry):
        body(lax.rem(me + offset_of(step, count), count))
        return carry

    lax.fori_loop(0, count - 1, one, 0)


def wait_bytes(ref, sem):
    pltpu.make_async_copy(ref, ref, sem).wait()


def rows_of(index, size):
    return pl.ds(pl.multiple_of(index * size, size), size)


def parts_of(value):
    high = value.astype(jnp.bfloat16).astype(jnp.float32)
    rest = value - high
    middle = rest.astype(jnp.bfloat16).astype(jnp.float32)
    return high, middle, rest - middle


def contract(a, b, dims, **kw):
    return lax.dot_general(a, b, (dims, ((), ())), preferred_element_type=jnp.float32, **kw)


def step_kernel(
    members,
    slabs,
    state_hbm,
    coef_hbm,
    solve_hbm,
    land_hbm,
    target_hbm,
    w_in_hbm,
    bias_in_hbm,
    land_weight_hbm,
    w_out_hbm,
    bias_out_hbm,
    code_ref,
    bounds_ref,
    state_ref,
    total_ref,
    state_in,
    coef_ref,
    solve_ref,
    land_ref,
    target_ref,
    w_in_ref,
    bias_in_ref,
    land_weight_ref,
    w_out_ref,
    bias_out_ref,
    field,
    north,
    send,
    recv,
    solve_s,
    w_aug,
    w_back,
    x_aug,
    shift,
    z_s,
    slope,
    dy_s,
    da_s,
    back,
    back_in,
    grads,
    pair_in,
    pair_sum,
    plane_in,
    near_in,
    far_in,
    piece,
    level_out,
    level_in,
    field_in,
    half_all,
    twin_all,
    load_sem,
    chunk_sem,
    send_sem,
    recv_sem,
):
    ens, slab = lax.axis_index("ens"), lax.axis_index("slab")
    lats, lons = state_in.shape
    levels, hidden = w_in_ref.shape
    blocks = lons // LANES
    chunks, pad, width = x_aug.shape
    wide = width // LANES
    extra = pad - levels
    hb = min(128, hidden)
    core = lax.rem(slab, 2)
    twin = slab + 1 - 2 * core
    half_slabs = slabs // 2
    upper = slab // half_slabs
    other = lax.rem(slab + half_slabs, slabs)
    column = lax.rem(slab, half_slabs)
    near = near_in.shape[0] // piece.shape[0]
    far = far_in.shape[0] // piece.shape[0]
    heights = near * far
    height = column // 2
    plane = ens * 2 + upper
    planes = members * 2
    rows = piece.shape[0]
    half = hidden // 2
    highest = lax.Precision.HIGHEST

    loads = [
        pltpu.make_async_copy(src, dst, load_sem.at[k])
        for k, (src, dst) in enumerate(
            (
                (state_hbm, state_in),
                (coef_hbm, coef_ref),
                (solve_hbm, solve_ref),
                (land_hbm, land_ref),
                (target_hbm, target_ref),
                (w_in_hbm, w_in_ref),
                (bias_in_hbm, bias_in_ref),
                (land_weight_hbm, land_weight_ref),
                (w_out_hbm, w_out_ref),
                (bias_out_hbm, bias_out_ref),
            )
        )
    ]
    for load in loads:
        load.start()

    barrier = pltpu.get_barrier_semaphore()

    def greet(device):
        pl.semaphore_signal(barrier, inc=1, device_id=device, device_id_type=MESH)

    def greet_member(e):
        greet((e, slab))
        greet((e, other))

    for_peers(slabs, slab, lambda d: greet((ens, d)))
    for_peers(members, ens, greet_member)

    def put(k, src, dst, device, arrived=None):
        pltpu.make_async_remote_copy(
            src_ref=src,
            dst_ref=dst,
            send_sem=send_sem.at[k],
            recv_sem=recv_sem.at[k] if arrived is None else arrived,
            device_id=device,
            device_id_type=MESH,
        ).start()

    mult = lax.rem(code_ref[0], 251) + 2
    base = lax.rem(slab * (lats * lons), PRIME)
    field[0:8, :] = jnp.zeros((8, lons), jnp.float32)
    field[8 + lats : 16 + lats, :] = jnp.zeros((8, lons), jnp.float32)
    loads[0].wait()
    for start in range(0, lats, 8):
        field[8 + start : 16 + start, :] = state_in[start : start + 8, :] + noise(
            mult, base, start, 8, lons
        )
    loads[1].wait()
    prepare_north(coef_ref, north)

    def emit_send(start, count, value):
        for j in range(blocks):
            send[pl.ds(start * blocks + j, count, stride=blocks), :] = value[
                :, j * LANES : (j + 1) * LANES
            ]

    diffuse(field, coef_ref, north, emit_send)

    def chunk_of(step):
        return lax.rem(ens // 2 + 1 + step, chunks)

    def some_rows(device, step):
        return pl.ds(device * blocks + chunk_of(step) * wide, wide)

    pl.semaphore_wait(barrier, slabs - 1 + 2 * (members - 1))
    for step in range(chunks):
        for_peers(
            slabs,
            slab,
            lambda d: put(
                0,
                send.at[some_rows(d, step)],
                recv.at[some_rows(slab, step)],
                (ens, d),
                chunk_sem.at[step],
            ),
        )
    recv[rows_of(slab, blocks), :] = send[rows_of(slab, blocks), :]

    for load in loads[2:]:
        load.wait()
    row = lax.broadcasted_iota(jnp.int32, (levels, levels), 0)
    col = lax.broadcasted_iota(jnp.int32, (levels, levels), 1)
    row_block = jnp.zeros((levels, levels), jnp.int32)
    col_block = jnp.zeros((levels, levels), jnp.int32)
    for j in range(1, bounds_ref.shape[0] - 1):
        row_block += (row >= bounds_ref[j]).astype(jnp.int32)
        col_block += (col >= bounds_ref[j]).astype(jnp.int32)
    solve_s[...] = jnp.where(row_block == col_block, solve_ref[...], 0.0)
    bias = parts_of(bias_in_ref[...] * 0.5)
    land_w = parts_of(land_weight_ref[...] * 0.5)
    land = land_ref[...].astype(jnp.float32)
    extra_row = lax.broadcasted_iota(jnp.int32, (extra, hidden), 0)
    tail = jnp.zeros((extra, hidden), jnp.float32)
    for k, part in enumerate(bias + land_w):
        tail = jnp.where(extra_row == k, part, tail)
    whole = jnp.concatenate([w_in_ref[...].astype(jnp.float32) * 0.5, tail], axis=0)
    w_aug[...] = whole.T.astype(jnp.bfloat16)
    spread = jnp.concatenate(
        [w_out_ref[...].astype(jnp.float32) * 0.5, jnp.zeros((extra, hidden), jnp.float32)], axis=0
    )
    w_back[...] = spread.T.astype(jnp.bfloat16)
    lon_row = lax.broadcasted_iota(jnp.int32, (extra, lons), 0)
    ones = jnp.where(lon_row < 3, 1.0, jnp.where(lon_row < 6, land, 0.0)).astype(jnp.bfloat16)
    bias_col = jnp.sum(jnp.where(row == col, bias_out_ref[...], 0.0), axis=1, keepdims=True)
    for c in range(chunks):
        here = slice(c * width, (c + 1) * width)
        x_aug[c, levels:, :] = ones[:, here]
        shift[c] = bias_col - target_ref[:, here].astype(jnp.float32)
    dy_s[levels:, :] = jnp.zeros((extra, width), jnp.bfloat16)
    grads[...] = jnp.zeros(grads.shape, jnp.float32)

    def column_chunk(step, carry):
        c = chunk_of(step)
        wait_bytes(recv.at[pl.ds(0, (slabs - 1) * wide)], chunk_sem.at[step])
        h = jnp.concatenate(
            [recv[pl.ds(c * wide + j, levels, stride=blocks), :] for j in range(wide)], axis=1
        )
        x = contract(solve_s[...], h, ((1,), (0,)), precision=highest).astype(jnp.bfloat16)
        x_aug[c, 0:levels, :] = x
        x_all = x_aug[c]
        for k in range(0, hidden, hb):
            pre = contract(w_aug[k : k + hb, :], x_all, ((1,), (0,)))
            t = jnp.tanh(pre)
            both = pre * t
            z_s[k : k + hb, :] = (pre + both).astype(jnp.bfloat16)
            slope[k : k + hb, :] = (1.0 + t) * (1.0 + pre - both)
        out = contract(w_out_ref[...], z_s[...], ((1,), (0,)))
        dy = ((out + shift[c]) * (1.0 / members)).astype(jnp.bfloat16)
        dy_s[0:levels, :] = dy
        dy_all = dy_s[...]
        for k in range(0, hidden, hb):
            dz = contract(w_back[k : k + hb, :], dy_all, ((1,), (0,)))
            da_s[k : k + hb, :] = (dz * slope[k : k + hb, :]).astype(jnp.bfloat16)
        dx = contract(w_in_ref[...], da_s[...], ((1,), (0,)))
        dh = contract(solve_s[...], dx, ((0,), (0,)), precision=highest)
        for j in range(wide):
            e = c * wide + j
            back[rows_of(e, levels), :] = dh[:, j * LANES : (j + 1) * LANES]

            @pl.when(e != ens)
            def _():
                put(1, back.at[rows_of(e, levels)], back_in.at[rows_of(ens, levels)], (e, slab))

        for k in range(2):
            part = slice(k * half, (k + 1) * half)
            grads[k, 0:levels, :] += contract(x, da_s[part, :], ((1,), (1,)))
            grads[k, levels:, :] += contract(dy, z_s[part, :], ((1,), (1,)))
        return carry

    lax.fori_loop(0, chunks, column_chunk, 0)

    put(2, grads.at[1 - core], pair_in, (ens, twin))
    back_in[rows_of(ens, levels), :] = back[rows_of(ens, levels), :]
    wait_bytes(pair_in, recv_sem.at[2])
    pair_sum[...] = grads[core] + pair_in[...]

    def plane_device(q):
        return (q // 2, lax.rem(q, 2) * half_slabs + column)

    for_peers(
        planes,
        plane,
        lambda q: put(
            3, pair_sum.at[rows_of(q, rows)], plane_in.at[rows_of(plane, rows)], plane_device(q)
        ),
    )
    plane_in[rows_of(plane, rows), :] = pair_sum[rows_of(plane, rows), :]
    wait_bytes(back_in.at[pl.ds(0, (members - 1) * levels)], recv_sem.at[1])
    summed = back_in[0:levels, :]
    for e in range(1, members):
        summed += back_in[e * levels : (e + 1) * levels, :]
    level_out[...] = summed
    for_peers(
        slabs,
        slab,
        lambda d: put(4, level_out.at[pl.ds(d, 1)], level_in.at[pl.ds(slab, 1)], (ens, d)),
    )
    level_in[pl.ds(slab, 1), :] = level_out[pl.ds(slab, 1), :]
    wait_bytes(plane_in.at[pl.ds(0, (planes - 1) * rows)], recv_sem.at[3])
    summed = plane_in[0:rows, :]
    for q in range(1, planes):
        summed += plane_in[q * rows : (q + 1) * rows, :]

    def height_device(h):
        return (ens, upper * half_slabs + 2 * h + core)

    spot, group = lax.rem(height, near), height // near
    near_in[rows_of(spot, rows), :] = summed
    mine = rows_of(spot, rows)
    for k in range(1, near):
        peer = group * near + lax.rem(spot + k, near)
        put(5, near_in.at[mine], near_in.at[mine], height_device(peer))
    wait_bytes(near_in.at[pl.ds(0, (near - 1) * rows)], recv_sem.at[5])
    summed = near_in[0:rows, :]
    for k in range(1, near):
        summed += near_in[k * rows : (k + 1) * rows, :]
    from_far = rows_of(group, rows)
    far_in[from_far, :] = summed
    for k in range(1, far):
        peer = lax.rem(height + k * near, heights)
        put(6, far_in.at[from_far], far_in.at[from_far], height_device(peer))
    wait_bytes(level_in.at[pl.ds(0, slabs - 1)], recv_sem.at[4])
    for_peers(
        members, ens, lambda e: put(7, level_in, field_in.at[rows_of(ens, lats)], (e, slab))
    )
    field_in[rows_of(ens, lats), :] = level_in[...]
    wait_bytes(far_in.at[pl.ds(0, (far - 1) * rows)], recv_sem.at[6])
    summed = far_in[0:rows, :]
    for k in range(1, far):
        summed += far_in[k * rows : (k + 1) * rows, :]
    piece[...] = summed
    for_peers(
        planes,
        plane,
        lambda q: put(8, piece, half_all.at[rows_of(plane, rows)], plane_device(q)),
    )
    half_all[rows_of(plane, rows), :] = piece[...]
    wait_bytes(field_in.at[pl.ds(0, (members - 1) * lats)], recv_sem.at[7])
    for e in range(members):
        field[8 : 8 + lats, e * LANES : (e + 1) * LANES] = field_in[e * lats : (e + 1) * lats, :]

    def emit_state(start, count, value):
        state_ref[start : start + count, :] = value

    diffuse(field, coef_ref, north, emit_state)
    wait_bytes(half_all.at[pl.ds(0, (planes - 1) * rows)], recv_sem.at[8])
    put(9, half_all, twin_all, (ens, twin))
    total_ref[core] = half_all[...]
    wait_bytes(send.at[pl.ds(0, (slabs - 1) * blocks)], send_sem.at[0])
    wait_bytes(back.at[pl.ds(0, (members - 1) * levels)], send_sem.at[1])
    wait_bytes(pair_in, send_sem.at[2])
    wait_bytes(plane_in.at[pl.ds(0, (planes - 1) * rows)], send_sem.at[3])
    wait_bytes(level_in.at[pl.ds(0, slabs - 1)], send_sem.at[4])
    wait_bytes(near_in.at[pl.ds(0, (near - 1) * rows)], send_sem.at[5])
    wait_bytes(far_in.at[pl.ds(0, (far - 1) * rows)], send_sem.at[6])
    wait_bytes(field_in.at[pl.ds(0, (members - 1) * lats)], send_sem.at[7])
    wait_bytes(half_all.at[pl.ds(0, (planes - 1) * rows)], send_sem.at[8])
    wait_bytes(twin_all, recv_sem.at[9])
    total_ref[1 - core] = twin_all[...]
    wait_bytes(twin_all, send_sem.at[9])


def finish_kernel(total_ref, grad_ref, in_ref, out_ref, state_ref):
    levels, hidden = in_ref.shape
    half = hidden // 2
    for ref, first in ((in_ref, 0), (out_ref, levels)):
        square = jnp.zeros((1, 1), jnp.float32)
        for k in range(2):
            grad = total_ref[k, first : first + levels, :]
            square += jnp.sum(jnp.sum(grad * grad, axis=0, keepdims=True), axis=1, keepdims=True)
        scale = 1.0 / jnp.sqrt(square * (1.0 / (levels * hidden)) + 1e-06)
        for k in range(2):
            ref[:, k * half : (k + 1) * half] = total_ref[k, first : first + levels, :] * scale
    state_ref[...] = grad_ref[...]


def on_device(
    members,
    slabs,
    state,
    face_coefs,
    codes,
    acoustic_inv,
    bounds,
    land_mask,
    target,
    w_in,
    bias_in,
    land_weight,
    w_out,
    bias_out,
):
    _, lats, lons = state.shape
    levels, hidden = w_in.shape
    blocks = lons // LANES
    f32, bf16 = jnp.float32, jnp.bfloat16
    vmem = pl.BlockSpec(memory_space=pltpu.VMEM)
    smem = pl.BlockSpec(memory_space=pltpu.SMEM)
    hbm = pl.BlockSpec(memory_space=pltpu.HBM)
    like = jax.ShapeDtypeStruct
    dma = pltpu.SemaphoreType.DMA
    pad = 2 * levels if levels >= 64 else levels + 16
    width = 2 * LANES
    chunks = lons // width
    half = hidden // 2
    planes = 2 * members
    rows = 2 * levels // planes
    heights = slabs // 4
    near = 4 if heights >= 16 else 2
    far = heights // near
    fetched = (
        state.reshape(lats, lons),
        face_coefs.reshape(2, lats, lons),
        acoustic_inv.reshape(levels, levels),
        land_mask,
        target.reshape(levels, lons),
        w_in,
        bias_in.reshape(1, hidden),
        land_weight.reshape(1, hidden),
        w_out.T,
        bias_out.reshape(1, levels),
    )
    grad_state, total = pl.pallas_call(
        functools.partial(step_kernel, members, slabs),
        out_shape=(like((lats, lons), f32), like((2, 2 * levels, half), f32)),
        in_specs=[hbm] * len(fetched) + [smem, smem],
        out_specs=(vmem, vmem),
        scratch_shapes=[pltpu.VMEM(v.shape, v.dtype) for v in fetched]
        + [
            pltpu.VMEM((lats + 16, lons), f32),
            pltpu.VMEM((lats + 8, lons), f32),
            pltpu.VMEM((lats * blocks, LANES), f32),
            pltpu.VMEM((levels * blocks, LANES), f32),
            pltpu.VMEM((levels, levels), f32),
            pltpu.VMEM((hidden, pad), bf16),
            pltpu.VMEM((hidden, pad), bf16),
            pltpu.VMEM((chunks, pad, width), bf16),
            pltpu.VMEM((chunks, levels, width), f32),
            pltpu.VMEM((hidden, width), bf16),
            pltpu.VMEM((hidden, width), f32),
            pltpu.VMEM((pad, width), bf16),
            pltpu.VMEM((hidden, width), bf16),
            pltpu.VMEM((members * levels, LANES), f32),
            pltpu.VMEM((members * levels, LANES), f32),
            pltpu.VMEM((2, 2 * levels, half), f32),
            pltpu.VMEM((2 * levels, half), f32),
            pltpu.VMEM((2 * levels, half), f32),
            pltpu.VMEM((planes * rows, half), f32),
            pltpu.VMEM((near * rows, half), f32),
            pltpu.VMEM((far * rows, half), f32),
            pltpu.VMEM((rows, half), f32),
            pltpu.VMEM((levels, LANES), f32),
            pltpu.VMEM((lats, LANES), f32),
            pltpu.VMEM((members * lats, LANES), f32),
            pltpu.VMEM((2 * levels, half), f32),
            pltpu.VMEM((2 * levels, half), f32),
            dma((len(fetched),)),
            dma((chunks,)),
            dma((10,)),
            dma((10,)),
        ],
        compiler_params=pltpu.CompilerParams(
            collective_id=0, has_side_effects=True, vmem_limit_bytes=40 * 1024 * 1024
        ),
    )(*fetched, codes, bounds)
    upd_in, upd_out, grad_state = pl.pallas_call(
        finish_kernel,
        out_shape=(
            like((levels, hidden), f32),
            like((levels, hidden), f32),
            like((lats, lons), f32),
        ),
        in_specs=[vmem] * 2,
        out_specs=(vmem,) * 3,
        compiler_params=pltpu.CompilerParams(vmem_limit_bytes=16 * 1024 * 1024),
    )(total, grad_state)
    return upd_in, upd_out.T, grad_state.reshape(state.shape)


def solution(mesh):
    placed = (
        P("slab", None, None),
        P(None, "slab", None, None),
        P("ens"),
        P("slab", None, None),
        P(),
        P("slab", None),
        P(None, "slab", None),
        P(),
        P(),
        P(),
        P(),
        P(),
    )
    return jax.shard_map(
        functools.partial(on_device, mesh.shape["ens"], mesh.shape["slab"]),
        mesh=mesh,
        in_specs=placed,
        out_specs=(P(), P(), P("slab", None, None)),
        check_vma=False,
    )
```

time: 653 us -> 75.2 us (0.12)
  waiting for transfers between devices: 562 us -> 0 us
  Pallas kernels: 0 us -> 67.5 us
  other arithmetic: 27.4 us -> 0 us
  starting transfers between devices: 24.2 us -> 0 us
  between operations: 17.9 us -> 1.34 us
  matrix products: 9.94 us -> 0 us
    psum x2 -> x0, waiting for transfers between devices: 538 us -> none  [the longest x1 461 us: on_device(): g_in, g_out = lax.psum((g_in, g_out), ('ens', 'slab'))]
    pallas_call x0 -> x2, Pallas kernels: none -> 67.5 us  [the longest x1 66.4 us: on_device(): pl.pallas_call(functools.partial(step_kernel, members, slabs), out_shape=...]
    all_to_all x2 -> x0, starting transfers between devices: 24 us -> none  [the longest x1 19.8 us: on_device(): lax.all_to_all(fresh, 'slab', split_axis=1, concat_axis=0, tiled=True)]
    all_to_all x2 -> x0, waiting for transfers between devices: 23.6 us -> none  [the longest x1 23.6 us: on_device(): lax.all_to_all(fresh, 'slab', split_axis=1, concat_axis=0, tiled=True)]
    dot_general x8 -> x0, matrix products: 9.94 us -> none  [the longest x1 2.78 us: column_step(): lax.dot_general(hidden, d_out, (((1,), (1,)), ((), ())), preferred_elemen...]
    sub x4 -> x0, other arithmetic: 8.35 us -> none  [the longest x2 6.83 us: diffuse(): return field + flux_x - jnp.roll(flux_x, 1, axis=2) + flux_y - lower]
    mul x4 -> x0, other arithmetic: 7.5 us -> none  [the longest x2 7.23 us: diffuse(): flux_x = east * (jnp.roll(field, -1, axis=2) - field)]
  transfers between devices with their start and end apart: 4 -> 0, of which waited for: 3 -> 0; matrix products, arithmetic and copies ran while one was open for 2% -> 0% of each run, Pallas kernels for 0% -> 0%
where the time goes in v2:
time: 75.2 us; the launch traced here: 74.8 us
  Pallas kernels  67.5 us (90%)
  local copies, waits for them, and re-layouts  6.05 us (8%)
  between operations  1.34 us (2%)
    pallas_call x1, Pallas kernels, on_device(): pl.pallas_call(functools.partial(step_kernel, members, slabs), out_shape=...  66.4 us
    unnamed x22, local copies, waits for them, and re-layouts  6.05 us

profile of v2, /device:TPU:1, one launch (start us, length us, event | category | flops | bytes accessed | tf_op | source)
XLA Modules:
  0.0 74.8 jit_solution(10574668057135566995)
XLA Ops:
  1.3 0.0 copy-start.8
  1.3 0.0 copy-start.7
  1.3 0.0 copy-start.6
  1.3 0.0 copy-start.9
  1.3 0.0 copy-start.10
  1.3 0.6 copy-done.8
  2.0 0.0 copy-done.7
  2.0 0.0 copy-done.6
  2.0 0.0 copy-done.9
  2.0 0.0 copy-done.10
  2.0 0.0 copy-start
  2.0 0.9 %copy-done = f32[1,64,1024]{2,1,0:T(8,128)S(1)} copy-done((f32[1,64,1024]{2,1,0:T(8,128)S(1)}, f32[1,64,1024]{2,1,0:T(8,128)}, u32[]{:S(2)}) %copy-start) | copy-done | bytes 262168
  3.0 0.0 copy-start.1
  3.0 0.9 %copy-done.1 = bf16[2,1,64,1024]{3,2,1,0:T(8,128)(2,1)S(1)} copy-done((bf16[2,1,64,1024]{3,2,1,0:T(8,128)(2,1)S(1)}, bf16[2,1,64,1024]{3,2,1,0:T(8,128)(2,1)}, u32[]{:S(2)}) %copy-start.1) | copy-done | bytes 262168
  3.9 0.0 copy-start.2
  3.9 0.9 %copy-done.2 = bf16[64,1,1024]{2,0,1:T(8,128)(2,1)S(1)} copy-done((bf16[64,1,1024]{2,0,1:T(8,128)(2,1)S(1)}, bf16[64,1,1024]{2,0,1:T(8,128)(2,1)}, u32[]{:S(2)}) %copy-start.2) | copy-done | bytes 131096
  4.8 0.0 copy-start.3
  4.8 0.9 %copy-done.3 = bf16[64,1024]{1,0:T(8,128)(2,1)S(1)} copy-done((bf16[64,1024]{1,0:T(8,128)(2,1)S(1)}, bf16[64,1024]{1,0:T(8,128)(2,1)}, u32[]{:S(2)}) %copy-start.3) | copy-done | bytes 131096
  5.7 0.0 copy-start.4
  5.7 0.9 %copy-done.4 = bf16[1024,64]{0,1:T(8,128)(2,1)S(1)} copy-done((bf16[1024,64]{0,1:T(8,128)(2,1)S(1)}, bf16[1024,64]{0,1:T(8,128)(2,1)}, u32[]{:S(2)}) %copy-start.4) | copy-done | bytes 131096
  6.6 0.0 copy-start.5
  6.6 0.8 %copy-done.5 = f32[1,64,64]{2,1,0:T(8,128)S(1)} copy-done((f32[1,64,64]{2,1,0:T(8,128)S(1)}, f32[1,64,64]{2,1,0:T(8,128)}, u32[]{:S(2)}) %copy-start.5) | copy-done | bytes 16408
  7.4 66.4 %shard_map.139 = (f32[64,1024]{1,0:T(8,128)S(1)}, f32[2,128,512]{2,1,0:T(8,128)S(1)}) custom-call(f32[64,1024]{1,0:T(8,128)S(1)} %bitcast.10, bf16[2,64,1024]{2,1,0:T(8,128)(2,1)S(1)} %bitcast.11, f32[64,64]{1,0:T(8,128)S(1)} %bitcast.14, s32[1,1024]{1,0:T(1,128)S(1)} %copy-done.6, bf16[64,1024]{1,0:T(8,128)(2,1)S(1)} %bitcast.12, ...), custom_call_target="tpu_custom_call" | custom-call | tf_op jit(solution)/shard_map/pallas_call | solution.py:480
  73.8 1.0 %shard_map.140 = (f32[64,1024]{1,0:T(8,128)}, f32[64,1024]{1,0:T(8,128)}, f32[64,1024]{1,0:T(8,128)}) custom-call(f32[2,128,512]{2,1,0:T(8,128)S(1)} %get-tuple-element.8.total_ref, f32[64,1024]{1,0:T(8,128)S(1)} %get-tuple-element.9.grad_ref), custom_call_target="tpu_custom_call" | custom-call | tf_op jit(solution)/shard_map/pallas_call | solution.py:523
Async XLA Ops:
  1.3 0.7 copy-start.8
  1.3 0.7 copy-start.7
  1.3 0.7 copy-start.6
  1.3 0.7 copy-start.9
  1.3 0.7 copy-start.10
  2.0 1.0 %copy-start = (f32[1,64,1024]{2,1,0:T(8,128)S(1)}, f32[1,64,1024]{2,1,0:T(8,128)}, u32[]{:S(2)}) copy-start(f32[1,64,1024]{2,1,0:T(8,128)} %param.12) | copy-start | bytes 786436
  3.0 0.9 %copy-start.1 = (bf16[2,1,64,1024]{3,2,1,0:T(8,128)(2,1)S(1)}, bf16[2,1,64,1024]{3,2,1,0:T(8,128)(2,1)}, u32[]{:S(2)}) copy-start(bf16[2,1,64,1024]{3,2,1,0:T(8,128)(2,1)} %param.13) | copy-start | bytes 786436
  3.9 0.9 %copy-start.2 = (bf16[64,1,1024]{2,0,1:T(8,128)(2,1)S(1)}, bf16[64,1,1024]{2,0,1:T(8,128)(2,1)}, u32[]{:S(2)}) copy-start(bf16[64,1,1024]{2,0,1:T(8,128)(2,1)} %param.18) | copy-start | bytes 393220
  4.8 0.9 %copy-start.3 = (bf16[64,1024]{1,0:T(8,128)(2,1)S(1)}, bf16[64,1024]{1,0:T(8,128)(2,1)}, u32[]{:S(2)}) copy-start(bf16[64,1024]{1,0:T(8,128)(2,1)} %w_in_hbm.1) | copy-start | bytes 393220
  5.7 0.9 %copy-start.4 = (bf16[1024,64]{0,1:T(8,128)(2,1)S(1)}, bf16[1024,64]{0,1:T(8,128)(2,1)}, u32[]{:S(2)}) copy-start(bf16[1024,64]{0,1:T(8,128)(2,1)} %param.22) | copy-start | bytes 393220
  6.6 0.8 %copy-start.5 = (f32[1,64,64]{2,1,0:T(8,128)S(1)}, f32[1,64,64]{2,1,0:T(8,128)}, u32[]{:S(2)}) copy-start(f32[1,64,64]{2,1,0:T(8,128)} %param.15) | copy-start | bytes 49156

commit v3 on v2

--- a/solution.py
+++ b/solution.py
@@ -56,6 +56,7 @@
 
 
 def offset_of(step, count):
+    step = count - 2 - step
     half = step // 2 + 1
     return jnp.where(step % 2 == 0, half, count - half)
 
@@ -102,8 +103,8 @@
     bias_out_hbm,
     code_ref,
     bounds_ref,
-    state_ref,
-    total_ref,
+    state_hbm_out,
+    total_hbm,
     state_in,
     coef_ref,
     solve_ref,
@@ -140,9 +141,10 @@
     level_in,
     field_in,
     half_all,
-    twin_all,
     load_sem,
+    store_sem,
     chunk_sem,
+    plane_sem,
     send_sem,
     recv_sem,
 ):
@@ -286,7 +288,15 @@
     dy_s[levels:, :] = jnp.zeros((extra, width), jnp.bfloat16)
     grads[...] = jnp.zeros(grads.shape, jnp.float32)
 
-    def column_chunk(step, carry):
+    def gradient(k, x, dy):
+        part = rows_of(k, half)
+        grads[k, 0:levels, :] += contract(x, da_s[part, :], ((1,), (1,)))
+        grads[k, levels:, :] += contract(dy, z_s[part, :], ((1,), (1,)))
+
+    def to_member(e):
+        put(1, back.at[rows_of(e, levels)], back_in.at[rows_of(ens, levels)], (e, slab))
+
+    def column_chunk(step, last):
         c = chunk_of(step)
         wait_bytes(recv.at[pl.ds(0, (slabs - 1) * wide)], chunk_sem.at[step])
         h = jnp.concatenate(
@@ -308,25 +318,27 @@
         for k in range(0, hidden, hb):
             dz = contract(w_back[k : k + hb, :], dy_all, ((1,), (0,)))
             da_s[k : k + hb, :] = (dz * slope[k : k + hb, :]).astype(jnp.bfloat16)
+        if last:
+            gradient(1 - core, x, dy)
+            put(2, grads.at[1 - core], pair_in, (ens, twin))
         dx = contract(w_in_ref[...], da_s[...], ((1,), (0,)))
         dh = contract(solve_s[...], dx, ((0,), (0,)), precision=highest)
         for j in range(wide):
             e = c * wide + j
             back[rows_of(e, levels), :] = dh[:, j * LANES : (j + 1) * LANES]
-
-            @pl.when(e != ens)
-            def _():
-                put(1, back.at[rows_of(e, levels)], back_in.at[rows_of(ens, levels)], (e, slab))
-
-        for k in range(2):
-            part = slice(k * half, (k + 1) * half)
-            grads[k, 0:levels, :] += contract(x, da_s[part, :], ((1,), (1,)))
-            grads[k, levels:, :] += contract(dy, z_s[part, :], ((1,), (1,)))
+            pl.when(e != ens)(functools.partial(to_member, e))
+        if last:
+            gradient(core, x, dy)
+        else:
+            gradient(0, x, dy)
+            gradient(1, x, dy)
+
+    def column_step(step, carry):
+        column_chunk(step, False)
         return carry
 
-    lax.fori_loop(0, chunks, column_chunk, 0)
-
-    put(2, grads.at[1 - core], pair_in, (ens, twin))
+    lax.fori_loop(0, chunks - 1, column_step, 0)
+    column_chunk(chunks - 1, True)
     back_in[rows_of(ens, levels), :] = back[rows_of(ens, levels), :]
     wait_bytes(pair_in, recv_sem.at[2])
     pair_sum[...] = grads[core] + pair_in[...]
@@ -389,20 +401,35 @@
     for_peers(
         planes,
         plane,
-        lambda q: put(8, piece, half_all.at[rows_of(plane, rows)], plane_device(q)),
+        lambda q: put(
+            8, piece, half_all.at[rows_of(plane, rows)], plane_device(q), plane_sem.at[plane]
+        ),
     )
     half_all[rows_of(plane, rows), :] = piece[...]
+
+    def to_twin(q):
+        at = rows_of(q, rows)
+        put(9, half_all.at[at], total_hbm.at[core, at], (ens, twin))
+
+    to_twin(plane)
     wait_bytes(field_in.at[pl.ds(0, (members - 1) * lats)], recv_sem.at[7])
     for e in range(members):
         field[8 : 8 + lats, e * LANES : (e + 1) * LANES] = field_in[e * lats : (e + 1) * lats, :]
 
     def emit_state(start, count, value):
-        state_ref[start : start + count, :] = value
+        state_in[start : start + count, :] = value
 
     diffuse(field, coef_ref, north, emit_state)
-    wait_bytes(half_all.at[pl.ds(0, (planes - 1) * rows)], recv_sem.at[8])
-    put(9, half_all, twin_all, (ens, twin))
-    total_ref[core] = half_all[...]
+    store_state = pltpu.make_async_copy(state_in, state_hbm_out, store_sem.at[0])
+    store_state.start()
+
+    def forward(q):
+        wait_bytes(half_all.at[rows_of(q, rows)], plane_sem.at[q])
+        to_twin(q)
+
+    for_peers(planes, plane, forward)
+    store_half = pltpu.make_async_copy(half_all, total_hbm.at[core], store_sem.at[1])
+    store_half.start()
     wait_bytes(send.at[pl.ds(0, (slabs - 1) * blocks)], send_sem.at[0])
     wait_bytes(back.at[pl.ds(0, (members - 1) * levels)], send_sem.at[1])
     wait_bytes(pair_in, send_sem.at[2])
@@ -412,9 +439,10 @@
     wait_bytes(far_in.at[pl.ds(0, (far - 1) * rows)], send_sem.at[6])
     wait_bytes(field_in.at[pl.ds(0, (members - 1) * lats)], send_sem.at[7])
     wait_bytes(half_all.at[pl.ds(0, (planes - 1) * rows)], send_sem.at[8])
-    wait_bytes(twin_all, recv_sem.at[9])
-    total_ref[1 - core] = twin_all[...]
-    wait_bytes(twin_all, send_sem.at[9])
+    wait_bytes(half_all, send_sem.at[9])
+    store_state.wait()
+    store_half.wait()
+    wait_bytes(total_hbm.at[1 - core], recv_sem.at[9])
 
 
 def finish_kernel(total_ref, grad_ref, in_ref, out_ref, state_ref):
@@ -481,7 +509,7 @@
         functools.partial(step_kernel, members, slabs),
         out_shape=(like((lats, lons), f32), like((2, 2 * levels, half), f32)),
         in_specs=[hbm] * len(fetched) + [smem, smem],
-        out_specs=(vmem, vmem),
+        out_specs=(hbm, hbm),
         scratch_shapes=[pltpu.VMEM(v.shape, v.dtype) for v in fetched]
         + [
             pltpu.VMEM((lats + 16, lons), f32),
@@ -510,14 +538,15 @@
             pltpu.VMEM((lats, LANES), f32),
             pltpu.VMEM((members * lats, LANES), f32),
             pltpu.VMEM((2 * levels, half), f32),
-            pltpu.VMEM((2 * levels, half), f32),
             dma((len(fetched),)),
+            dma((2,)),
             dma((chunks,)),
+            dma((planes,)),
             dma((10,)),
             dma((10,)),
         ],
         compiler_params=pltpu.CompilerParams(
-            collective_id=0, has_side_effects=True, vmem_limit_bytes=40 * 1024 * 1024
+            collective_id=0, has_side_effects=True, vmem_limit_bytes=56 * 1024 * 1024
         ),
     )(*fetched, codes, bounds)
     upd_in, upd_out, grad_state = pl.pallas_call(
@@ -529,7 +558,7 @@
         ),
         in_specs=[vmem] * 2,
         out_specs=(vmem,) * 3,
-        compiler_params=pltpu.CompilerParams(vmem_limit_bytes=16 * 1024 * 1024),
+        compiler_params=pltpu.CompilerParams(vmem_limit_bytes=56 * 1024 * 1024),
     )(total, grad_state)
     return upd_in, upd_out.T, grad_state.reshape(state.shape)
 

time: 75.2 us -> 69 us (0.918)
  local copies, waits for them, and re-layouts: 6.05 us -> 0 us
    unnamed x22 -> x0, local copies, waits for them, and re-layouts: 6.05 us -> none
    pallas_call x1, Pallas kernels: 1.03 us -> 2.14 us  [on_device(): pl.pallas_call(finish_kernel, out_shape=(like((levels, hidden), f32), lik...]
    pallas_call x1, Pallas kernels: 66.4 us -> 65.4 us  [on_device(): pl.pallas_call(functools.partial(step_kernel, members, slabs), out_shape=...]
where the time goes in v3:
time: 69 us; the launch traced here: 68.8 us
  Pallas kernels  67.5 us (98%)
  between operations  1.29 us (2%)
    pallas_call x1, Pallas kernels, on_device(): pl.pallas_call(functools.partial(step_kernel, members, slabs), out_shape=...  65.4 us
    pallas_call x1, Pallas kernels, on_device(): pl.pallas_call(finish_kernel, out_shape=(like((levels, hidden), f32), lik...  2.14 us

profile of v3, /device:TPU:1, one launch (start us, length us, event | category | flops | bytes accessed | tf_op | source)
XLA Modules:
  0.0 68.8 jit_solution(18314439309606516583)
XLA Ops:
  1.3 65.4 %shard_map.139 = (f32[64,1024]{1,0:T(8,128)}, f32[2,128,512]{2,1,0:T(8,128)}) custom-call(f32[64,1024]{1,0:T(8,128)} %bitcast.10, bf16[2,64,1024]{2,1,0:T(8,128)(2,1)} %bitcast.11, f32[64,64]{1,0:T(8,128)} %bitcast.14, s32[1,1024]{1,0:T(1,128)} %land_hbm.1, bf16[64,1024]{1,0:T(8,128)(2,1)} %bitcast.12, bf16[64,1024]{1,0:T(8,128)(2,1)} %w_in_hbm.1, ...), custom_call_target="tpu_custom_call" | custom-call | tf_op jit(solution)/shard_map/pallas_call | solution.py:508
  66.7 2.1 %shard_map.140 = (f32[64,1024]{1,0:T(8,128)}, f32[64,1024]{1,0:T(8,128)}, f32[64,1024]{1,0:T(8,128)}) custom-call(f32[2,128,512]{2,1,0:T(8,128)} %get-tuple-element.8.total_ref, f32[64,1024]{1,0:T(8,128)} %get-tuple-element.9.grad_ref), custom_call_target="tpu_custom_call" | custom-call | tf_op jit(solution)/shard_map/pallas_call | solution.py:552

commit v4 on v3

--- a/solution.py
+++ b/solution.py
@@ -55,18 +55,16 @@
         emit(start, step, here + flux_x - pltpu.roll(flux_x, 1, 1) + flux_y - lower)
 
 
-def offset_of(step, count):
-    step = count - 2 - step
-    half = step // 2 + 1
-    return jnp.where(step % 2 == 0, half, count - half)
-
-
 def for_peers(count, me, body):
-    def one(step, carry):
-        body(lax.rem(me + offset_of(step, count), count))
+    far = count // 2
+    body(lax.rem(me + far, count))
+
+    def both(step, carry):
+        body(lax.rem(me + (far - step), count))
+        body(lax.rem(me + (far + step), count))
         return carry
 
-    lax.fori_loop(0, count - 1, one, 0)
+    lax.fori_loop(1, far, both, 0)
 
 
 def wait_bytes(ref, sem):
@@ -410,6 +408,7 @@
     def to_twin(q):
         at = rows_of(q, rows)
         put(9, half_all.at[at], total_hbm.at[core, at], (ens, twin))
+        pltpu.make_async_copy(half_all.at[at], total_hbm.at[core, at], store_sem.at[1]).start()
 
     to_twin(plane)
     wait_bytes(field_in.at[pl.ds(0, (members - 1) * lats)], recv_sem.at[7])
@@ -428,8 +427,6 @@
         to_twin(q)
 
     for_peers(planes, plane, forward)
-    store_half = pltpu.make_async_copy(half_all, total_hbm.at[core], store_sem.at[1])
-    store_half.start()
     wait_bytes(send.at[pl.ds(0, (slabs - 1) * blocks)], send_sem.at[0])
     wait_bytes(back.at[pl.ds(0, (members - 1) * levels)], send_sem.at[1])
     wait_bytes(pair_in, send_sem.at[2])
@@ -441,22 +438,41 @@
     wait_bytes(half_all.at[pl.ds(0, (planes - 1) * rows)], send_sem.at[8])
     wait_bytes(half_all, send_sem.at[9])
     store_state.wait()
-    store_half.wait()
+    wait_bytes(half_all, store_sem.at[1])
     wait_bytes(total_hbm.at[1 - core], recv_sem.at[9])
 
 
-def finish_kernel(total_ref, grad_ref, in_ref, out_ref, state_ref):
-    levels, hidden = in_ref.shape
+def finish_kernel(
+    total_hbm, grad_hbm, in_hbm, out_hbm, state_hbm, total, done, state, load_sem, store_sem
+):
+    levels, hidden = in_hbm.shape
     half = hidden // 2
-    for ref, first in ((in_ref, 0), (out_ref, levels)):
+    load_state = pltpu.make_async_copy(grad_hbm, state, load_sem.at[2])
+    store_state = pltpu.make_async_copy(state, state_hbm, store_sem.at[2])
+    loads = []
+    for k in range(2):
+        at = pl.ds(k * levels, levels)
+        loads.append(pltpu.make_async_copy(total_hbm.at[:, at], total.at[:, at], load_sem.at[k]))
+        loads[k].start()
+    load_state.start()
+    stores = []
+    for n, ref in enumerate((in_hbm, out_hbm)):
+        first = n * levels
+        loads[n].wait()
         square = jnp.zeros((1, 1), jnp.float32)
         for k in range(2):
-            grad = total_ref[k, first : first + levels, :]
+            grad = total[k, first : first + levels, :]
             square += jnp.sum(jnp.sum(grad * grad, axis=0, keepdims=True), axis=1, keepdims=True)
         scale = 1.0 / jnp.sqrt(square * (1.0 / (levels * hidden)) + 1e-06)
         for k in range(2):
-            ref[:, k * half : (k + 1) * half] = total_ref[k, first : first + levels, :] * scale
-    state_ref[...] = grad_ref[...]
+            done[n, :, k * half : (k + 1) * half] = total[k, first : first + levels, :] * scale
+        stores.append(pltpu.make_async_copy(done.at[n], ref, store_sem.at[n]))
+        stores[n].start()
+    load_state.wait()
+    store_state.start()
+    for store in stores:
+        store.wait()
+    store_state.wait()
 
 
 def on_device(
@@ -479,7 +495,6 @@
     levels, hidden = w_in.shape
     blocks = lons // LANES
     f32, bf16 = jnp.float32, jnp.bfloat16
-    vmem = pl.BlockSpec(memory_space=pltpu.VMEM)
     smem = pl.BlockSpec(memory_space=pltpu.SMEM)
     hbm = pl.BlockSpec(memory_space=pltpu.HBM)
     like = jax.ShapeDtypeStruct
@@ -556,8 +571,15 @@
             like((levels, hidden), f32),
             like((lats, lons), f32),
         ),
-        in_specs=[vmem] * 2,
-        out_specs=(vmem,) * 3,
+        in_specs=[hbm] * 2,
+        out_specs=(hbm,) * 3,
+        scratch_shapes=[
+            pltpu.VMEM((2, 2 * levels, half), f32),
+            pltpu.VMEM((2, levels, hidden), f32),
+            pltpu.VMEM((lats, lons), f32),
+            dma((3,)),
+            dma((3,)),
+        ],
         compiler_params=pltpu.CompilerParams(vmem_limit_bytes=56 * 1024 * 1024),
     )(total, grad_state)
     return upd_in, upd_out.T, grad_state.reshape(state.shape)

time: 69 us -> 67.8 us (0.983)
  Pallas kernels: 67.5 us -> 66.4 us
    pallas_call x1, Pallas kernels: 65.4 us -> 64.3 us  [on_device(): pl.pallas_call(functools.partial(step_kernel, members, slabs), out_shape=...]
where the time goes in v4:
time: 67.8 us; the launch traced here: 67.7 us
  Pallas kernels  66.4 us (98%)
  between operations  1.29 us (2%)
    pallas_call x1, Pallas kernels, on_device(): pl.pallas_call(functools.partial(step_kernel, members, slabs), out_shape=...  64.3 us
    pallas_call x1, Pallas kernels, on_device(): pl.pallas_call(finish_kernel, out_shape=(like((levels, hidden), f32), lik...  2.08 us

profile of v4, /device:TPU:1, one launch (start us, length us, event | category | flops | bytes accessed | tf_op | source)
XLA Modules:
  0.0 67.7 jit_solution(15302227010573518697)
XLA Ops:
  1.3 64.3 %shard_map.139 = (f32[64,1024]{1,0:T(8,128)}, f32[2,128,512]{2,1,0:T(8,128)}) custom-call(f32[64,1024]{1,0:T(8,128)} %bitcast.10, bf16[2,64,1024]{2,1,0:T(8,128)(2,1)} %bitcast.11, f32[64,64]{1,0:T(8,128)} %bitcast.14, s32[1,1024]{1,0:T(1,128)} %land_hbm.1, bf16[64,1024]{1,0:T(8,128)(2,1)} %bitcast.12, bf16[64,1024]{1,0:T(8,128)(2,1)} %w_in_hbm.1, ...), custom_call_target="tpu_custom_call" | custom-call | tf_op jit(solution)/shard_map/pallas_call | solution.py:523
  65.6 2.1 %shard_map.140 = (f32[64,1024]{1,0:T(8,128)}, f32[64,1024]{1,0:T(8,128)}, f32[64,1024]{1,0:T(8,128)}) custom-call(f32[2,128,512]{2,1,0:T(8,128)} %get-tuple-element.8.total_hbm, f32[64,1024]{1,0:T(8,128)} %get-tuple-element.9.grad_hbm), custom_call_target="tpu_custom_call" | custom-call | tf_op jit(solution)/shard_map/pallas_call | solution.py:567

commit v5 on v4

--- a/solution.py
+++ b/solution.py
@@ -238,21 +238,6 @@
     def some_rows(device, step):
         return pl.ds(device * blocks + chunk_of(step) * wide, wide)
 
-    pl.semaphore_wait(barrier, slabs - 1 + 2 * (members - 1))
-    for step in range(chunks):
-        for_peers(
-            slabs,
-            slab,
-            lambda d: put(
-                0,
-                send.at[some_rows(d, step)],
-                recv.at[some_rows(slab, step)],
-                (ens, d),
-                chunk_sem.at[step],
-            ),
-        )
-    recv[rows_of(slab, blocks), :] = send[rows_of(slab, blocks), :]
-
     for load in loads[2:]:
         load.wait()
     row = lax.broadcasted_iota(jnp.int32, (levels, levels), 0)
@@ -285,6 +270,21 @@
         shift[c] = bias_col - target_ref[:, here].astype(jnp.float32)
     dy_s[levels:, :] = jnp.zeros((extra, width), jnp.bfloat16)
     grads[...] = jnp.zeros(grads.shape, jnp.float32)
+
+    pl.semaphore_wait(barrier, slabs - 1 + 2 * (members - 1))
+    for step in range(chunks):
+        for_peers(
+            slabs,
+            slab,
+            lambda d: put(
+                0,
+                send.at[some_rows(d, step)],
+                recv.at[some_rows(slab, step)],
+                (ens, d),
+                chunk_sem.at[step],
+            ),
+        )
+    recv[rows_of(slab, blocks), :] = send[rows_of(slab, blocks), :]
 
     def gradient(k, x, dy):
         part = rows_of(k, half)

time: 67.8 us -> 67.8 us (level)
  no operation moved by 1% of the time
where the time goes in v5:
time: 67.8 us; the launch traced here: 67.7 us
  Pallas kernels  66.4 us (98%)
  between operations  1.29 us (2%)
    pallas_call x1, Pallas kernels, on_device(): pl.pallas_call(functools.partial(step_kernel, members, slabs), out_shape=...  64.3 us
    pallas_call x1, Pallas kernels, on_device(): pl.pallas_call(finish_kernel, out_shape=(like((levels, hidden), f32), lik...  2.08 us

profile of v5, /device:TPU:1, one launch (start us, length us, event | category | flops | bytes accessed | tf_op | source)
XLA Modules:
  0.0 67.7 jit_solution(9865761660273383282)
XLA Ops:
  1.3 64.3 %shard_map.139 = (f32[64,1024]{1,0:T(8,128)}, f32[2,128,512]{2,1,0:T(8,128)}) custom-call(f32[64,1024]{1,0:T(8,128)} %bitcast.10, bf16[2,64,1024]{2,1,0:T(8,128)(2,1)} %bitcast.11, f32[64,64]{1,0:T(8,128)} %bitcast.14, s32[1,1024]{1,0:T(1,128)} %land_hbm.1, bf16[64,1024]{1,0:T(8,128)(2,1)} %bitcast.12, bf16[64,1024]{1,0:T(8,128)(2,1)} %w_in_hbm.1, ...), custom_call_target="tpu_custom_call" | custom-call | tf_op jit(solution)/shard_map/pallas_call | solution.py:523
  65.6 2.1 %shard_map.140 = (f32[64,1024]{1,0:T(8,128)}, f32[64,1024]{1,0:T(8,128)}, f32[64,1024]{1,0:T(8,128)}) custom-call(f32[2,128,512]{2,1,0:T(8,128)} %get-tuple-element.8.total_hbm, f32[64,1024]{1,0:T(8,128)} %get-tuple-element.9.grad_hbm), custom_call_target="tpu_custom_call" | custom-call | tf_op jit(solution)/shard_map/pallas_call | solution.py:567
